TPU v7x, 32 devices: a whole 2x2x4 slice. The times are simulated.
32 devices in a mesh: gx: 4 (over y, core), gy: 8 (over z, x).
Axes of the slice: x: 2, y: 2, z: 4, core: 2. Of those that a mesh axis runs over, the one named last changes fastest.
Arguments:
- patches: bfloat16 [2048, 1664], P(('gx', 'gy')), may hold values from -6 to 6
- prompt: bfloat16 [2560, 1664], P(('gx', 'gy')), may hold values from -6 to 6
- image_ids: int32 [4, 128], P('gx'), may hold values from 0 to 3, never falling along the last dimension, each value on 1 to 64 neighbouring positions
- positions: int32 [4, 128], P('gx'), may hold values from 0 to 639, as said below
- norm_gains: float32 [5, 1664], replicated, may hold values from 0.25 to 1.75
- vit_qkv: bfloat16 [1664, 4992], P('gx', 'gy'), may hold values from -0.24514517 to 0.24514517
- vit_out: bfloat16 [1664, 1664], P('gx', 'gy'), may hold values from -0.15625 to 0.15625
- vit_up: bfloat16 [1664, 8192], P('gx', 'gy'), may hold values from -0.15625 to 0.15625
- vit_down: bfloat16 [1664, 8192], P('gx', 'gy'), may hold values from -0.0625 to 0.0625
- merge_proj: bfloat16 [6656, 1664], P('gx', 'gy'), may hold values from -0.078125 to 0.078125
- dec_qkv: bfloat16 [1664, 4992], P('gx', 'gy'), may hold values from -0.24514517 to 0.24514517
- dec_out: bfloat16 [1664, 1664], P('gx', 'gy'), may hold values from -0.15625 to 0.15625
- dec_up: bfloat16 [1664, 8192], P('gx', 'gy'), may hold values from -0.15625 to 0.15625
- dec_down: bfloat16 [1664, 8192], P('gx', 'gy'), may hold values from -0.0625 to 0.0625
Outputs:
- decoded: bfloat16 [2560, 1664], P(('gx', 'gy'))
Inputs may be any that keep to these rules, and one draw needn't show every extreme that they name: `image_ids`: within each sequence image numbers never fall, and each of the 4 images has at least one merged row. Within each sequence the positions strictly increase.
All inputs are finite; a program needn't handle non-finite values.
Results may differ from a plain program's by a relative error of at most 0.03.
Values may be sent and summed in bfloat16 or wider, within the bound.
No kernel may reach another device: no remote copies, remote signals or barrier semaphores. Data moves between devices by JAX's collectives and lax.ppermute only.
A program may use at most 64 MiB of HBM per device.

v0:
```python
import math

import jax
import jax.numpy as jnp
from jax import lax
from jax.sharding import PartitionSpec as P

HEAD_DIM = 104


def layer_norm(rows, gain):
    values = rows.astype(jnp.float32)
    center = values - jnp.mean(values, axis=-1, keepdims=True)
    spread = jnp.mean(center * center, axis=-1, keepdims=True)
    return center * lax.rsqrt(spread + 1e-06) * gain


def rms_norm(rows, gain):
    values = rows.astype(jnp.float32)
    return values * lax.rsqrt(jnp.mean(values * values, axis=-1, keepdims=True) + 1e-06) * gain


def weight_block(weight):
    return lax.all_gather(weight, "gx", axis=0, tiled=True)


def spread_rows(rows, weight):

    def project(piece):
        if weight is None:
            return piece
        return jnp.dot(piece, weight, preferred_element_type=jnp.float32)

    return project(lax.all_gather(rows, "gy", axis=0, tiled=True))


def summed_rows(hidden, weight, local_rows):

    def term(start, count):
        return lax.dot_general(
            hidden, weight, (((1,), (1,)), ((), ())), preferred_element_type=jnp.float32
        )

    return lax.psum_scatter(
        term(jnp.int32(0), local_rows * lax.axis_size("gy")).astype(jnp.bfloat16),
        "gy",
        scatter_dimension=0,
        tiled=True,
    ).astype(jnp.float32)


def attend(joined, labels, causal):
    total = joined.shape[0]
    heads_here = joined.shape[1] // (3 * HEAD_DIM)
    grouped = joined.reshape(total, heads_here, 3, HEAD_DIM)
    query = grouped[:, :, 0]
    keys = grouped[:, :, 1]
    values = grouped[:, :, 2]
    block = 512 if total % 512 == 0 else total
    count = total // block
    scale = 1.0 / math.sqrt(HEAD_DIM)
    key_index = jnp.arange(total, dtype=jnp.int32)

    def one_block(inputs):
        query_block, number = inputs
        first = number * block
        scores = (
            jnp.einsum("qhe,khe->hqk", query_block, keys, preferred_element_type=jnp.float32)
            * scale
        )
        if causal:
            query_index = first + jnp.arange(block, dtype=jnp.int32)
            allowed = query_index[:, None] >= key_index[None, :]
        else:
            allowed = lax.dynamic_slice_in_dim(labels, first, block)[:, None] == labels[None, :]
        scores = jnp.where(allowed[None], scores, -1e30)
        top = jnp.max(scores, axis=-1, keepdims=True)
        weights = jnp.exp(scores - top)
        probs = (weights / jnp.sum(weights, axis=-1, keepdims=True)).astype(jnp.bfloat16)
        mixed = jnp.einsum("hqk,khe->qhe", probs, values, preferred_element_type=jnp.float32)
        return mixed.astype(jnp.bfloat16).reshape(block, heads_here * HEAD_DIM)

    blocks_out = lax.map(
        one_block,
        (query.reshape(count, block, heads_here, HEAD_DIM), jnp.arange(count, dtype=jnp.int32)),
    )
    return blocks_out.reshape(total, heads_here * HEAD_DIM)


def shards(
    patches,
    prompt,
    image_ids,
    positions,
    norm_gains,
    vit_qkv,
    vit_out,
    vit_up,
    vit_down,
    merge_proj,
    dec_qkv,
    dec_out,
    dec_up,
    dec_down,
):
    local = patches.shape[0]
    width = patches.shape[1]
    labels = jnp.repeat(image_ids[0], 4)
    enc_in = layer_norm(patches, norm_gains[0]).astype(jnp.bfloat16)
    enc_qkv = spread_rows(enc_in, weight_block(vit_qkv)).astype(jnp.bfloat16)
    enc_mix = attend(enc_qkv, labels, False)
    enc_mid = (
        patches.astype(jnp.float32) + summed_rows(enc_mix, weight_block(vit_out), local)
    ).astype(jnp.bfloat16)
    up_block = weight_block(vit_up)
    down_block = weight_block(vit_down)
    merge_block = weight_block(merge_proj)
    mid_all = spread_rows(enc_mid, None)
    normed = layer_norm(mid_all, norm_gains[1]).astype(jnp.bfloat16)
    enc_hidden = jax.nn.gelu(
        jnp.dot(normed, up_block, preferred_element_type=jnp.float32), approximate=False
    ).astype(jnp.bfloat16)
    term = lax.dot_general(
        enc_hidden, down_block, (((1,), (1,)), ((), ())), preferred_element_type=jnp.float32
    )
    enc_out = (
        mid_all.astype(jnp.float32) + lax.psum(term.astype(jnp.bfloat16), "gy").astype(jnp.float32)
    ).astype(jnp.bfloat16)
    windows = (
        layer_norm(enc_out, norm_gains[2])
        .astype(jnp.bfloat16)
        .reshape(enc_out.shape[0] // 4, 4 * width)
    )
    merged = jnp.dot(windows, merge_block, preferred_element_type=jnp.float32).astype(jnp.bfloat16)
    merged_all = lax.all_gather(merged, "gy", axis=1, tiled=True)
    seq_local = prompt.shape[0]
    seq_index = lax.axis_index("gy") * seq_local + jnp.arange(seq_local, dtype=jnp.int32)
    hits = positions[0][None, :] == seq_index[:, None]
    placed = jnp.dot(
        hits.astype(jnp.bfloat16), merged_all, preferred_element_type=jnp.float32
    ).astype(jnp.bfloat16)
    dec_in = jnp.where(jnp.any(hits, axis=1)[:, None], placed, prompt)
    dnormed = rms_norm(dec_in, norm_gains[3]).astype(jnp.bfloat16)
    dec_rows = spread_rows(dnormed, weight_block(dec_qkv)).astype(jnp.bfloat16)
    dec_mix = attend(dec_rows, None, True)
    dec_mid = (
        dec_in.astype(jnp.float32) + summed_rows(dec_mix, weight_block(dec_out), seq_local)
    ).astype(jnp.bfloat16)
    enormed = rms_norm(dec_mid, norm_gains[4]).astype(jnp.bfloat16)
    dec_hidden = jax.nn.gelu(spread_rows(enormed, weight_block(dec_up)), approximate=False).astype(
        jnp.bfloat16
    )
    return (
        dec_mid.astype(jnp.float32) + summed_rows(dec_hidden, weight_block(dec_down), seq_local)
    ).astype(jnp.bfloat16)


def solution(mesh):
    in_specs = (
        P(("gx", "gy"), None),
        P(("gx", "gy"), None),
        P("gx", None),
        P("gx", None),
        P(),
        P("gx", "gy"),
        P("gx", "gy"),
        P("gx", "gy"),
        P("gx", "gy"),
        P("gx", "gy"),
        P("gx", "gy"),
        P("gx", "gy"),
        P("gx", "gy"),
        P("gx", "gy"),
    )
    out_specs = P(("gx", "gy"), None)
    return jax.shard_map(shards, mesh=mesh, in_specs=in_specs, out_specs=out_specs, check_vma=False)
```

profile of v0, /device:TPU:0, one launch (start us, length us, event | category | flops | bytes accessed | tf_op | source)
XLA Modules:
  0.0 764.8 jit_solution(1164636283360438576)
XLA Ops:
  6.5 1.1 slice_reduce_fusion
  7.6 1.1 convert_reduce_fusion.2
  8.7 1.2 fusion.121
  9.9 1.8 fusion.123
  11.7 0.7 all-gather.14.cloned.1.call-update
  12.5 0.7 broadcast_in_dim.80
  13.2 0.1 eq.45
  13.3 0.2 broadcast_compare_fusion
  13.6 10.4 %all_gather.44 = bf16[1664,208]{1,0:T(8,128)(2,1)S(1)} all-gather(bf16[416,208]{1,0:T(8,128)(2,1)S(1)} %copy-done.4), channel_id=1, replica_groups=mesh['gx'=4,'gy'=8] {'gx'}, dimensions={0}, use_global_device_ids=true | all-gather | bytes 865280 | tf_op jit(solution)/shard_map/all_gather | solution.py:24
  24.0 35.8 %all-gather.12.cloned.1.call-done = bf16[512,1664]{1,0:T(8,128)(2,1)} async-done(((bf16[64,1664]{1,0:T(8,128)(2,1)}), bf16[512,1664]{1,0:T(8,128)(2,1)}) %all-gather.12.cloned.1.call-update) | async-done | bytes 1703952 | tf_op jit(solution)/shard_map/all_gather | solution.py:34
  59.8 23.3 %all-gather.14.cloned.1.call-done = bf16[1664,624]{1,0:T(8,128)(2,1)} async-done(((bf16[416,624]{1,0:T(8,128)(2,1)}), bf16[1664,624]{1,0:T(8,128)(2,1)}) %all-gather.14.cloned.1.call-update) | async-done | bytes 2076688 | tf_op jit(solution)/shard_map/all_gather | solution.py:24
  83.1 3.5 convolution_convert_fusion.6
  86.6 1.0 fusion.201
  87.6 1.3 convolution_convert_fusion.7
  88.9 1.9 convolution_convert_fusion.3
  90.8 0.0 all-gather.16.cloned.1.call-start
  90.9 66.0 %reduce-scatter.4.cloned.1.call-done = bf16[64,1664]{1,0:T(8,128)(2,1)} async-done(((bf16[512,1664]{1,0:T(8,128)(2,1)}), bf16[64,1664]{1,0:T(8,128)(2,1)}) %reduce-scatter.4.cloned.1.call-update) | async-done | bytes 213008 | tf_op jit(solution)/shard_map/reduce_scatter | solution.py:44
  156.8 1.7 fusion.124
  158.6 0.5 all-gather.18.cloned.1.call-update
  159.2 0.5 all-gather.20.cloned.1.call-update
  159.7 0.2 all-reduce.2.cloned.1.call-start
  159.9 43.4 %all-gather.16.cloned.1.call-done = bf16[512,1664]{1,0:T(8,128)(2,1)} async-done(((bf16[64,1664]{1,0:T(8,128)(2,1)}), bf16[512,1664]{1,0:T(8,128)(2,1)}) %all-gather.16.cloned.1.call-update) | async-done | bytes 1703952 | tf_op jit(solution)/shard_map/all_gather | solution.py:34
  203.3 1.9 convert_reduce_fusion
  205.2 0.1 copy-done
  205.2 0.6 fusion.6
  205.8 27.9 %all-gather.18.cloned.1.call-done = bf16[1664,1024]{1,0:T(8,128)(2,1)} async-done(((bf16[416,1024]{1,0:T(8,128)(2,1)}), bf16[1664,1024]{1,0:T(8,128)(2,1)}) %all-gather.18.cloned.1.call-update) | async-done | bytes 3407888 | tf_op jit(solution)/shard_map/all_gather | solution.py:24
  233.8 31.5 %all-gather.20.cloned.1.call-done = bf16[1664,1024]{1,0:T(8,128)(2,1)} async-done(((bf16[416,1024]{1,0:T(8,128)(2,1)}), bf16[1664,1024]{1,0:T(8,128)(2,1)}) %all-gather.20.cloned.1.call-update) | async-done | bytes 3407888 | tf_op jit(solution)/shard_map/all_gather | solution.py:24
  265.3 12.6 %convolution_convert_fusion.2 = bf16[512,1664]{1,0:T(8,128)(2,1)} fusion(bf16[1664,1024]{1,0:T(8,128)(2,1)} %all-gather.20.cloned.1.call-done, bf16[1664,1024]{1,0:T(8,128)(2,1)} %all-gather.18.cloned.1.call-done, bf16[512,1664]{1,0:T(8,128)(2,1)S(1)} %copy-done, f32[1664]{0:T(1024)S(1)} %get-tuple-element.32, f32[512]{0:T(512)S(1)} %add_rsqrt_fusion.1, ...), kind=kOutput, calls=%fused_computation.25 | convolution fusion | flops 3528851456 | bytes 10234368 | tf_op jit(solution)/shard_map/dot_general | solution.py:123
  277.9 0.0 all-gather.22.cloned.1.call-start
  278.0 0.7 all-gather.22.cloned.1.call-update
  278.7 0.7 all-gather.26.cloned.1.call-update
  279.4 0.3 all-gather.24.cloned.1.call-start
  279.7 0.2 compare_reduce_fusion
  279.9 90.6 %all-reduce.2.cloned.1.call-done = bf16[512,1664]{1,0:T(8,128)(2,1)} async-done(((bf16[512,1664]{1,0:T(8,128)(2,1)}), bf16[512,1664]{1,0:T(8,128)(2,1)}) %all-reduce.2.cloned.1.call-update) | async-done | bytes 1703952 | tf_op jit(solution)/shard_map/psum | solution.py:127
  370.5 2.1 convert_reduce_fusion.1
  372.6 0.8 fusion.9
  373.4 0.8 fusion.11
  374.2 1.2 reshape.140
  375.4 22.6 %all-gather.22.cloned.1.call-done = bf16[6656,208]{0,1:T(8,128)(2,1)} async-done(((bf16[1664,208]{0,1:T(8,128)(2,1)}), bf16[6656,208]{0,1:T(8,128)(2,1)}) %all-gather.22.cloned.1.call-update) | async-done | bytes 2768912 | tf_op jit(solution)/shard_map/all_gather | solution.py:24
  398.0 2.6 convolution_convert_fusion.8
  400.7 31.4 %all_gather.49 = bf16[128,1664]{0,1:T(8,128)(2,1)S(1)} all-gather(bf16[128,208]{0,1:T(8,128)(2,1)S(1)} %convolution_convert_fusion.8), channel_id=1, replica_groups=mesh['gx'=4,'gy'=8] {'gy'}, dimensions={1}, use_global_device_ids=true | all-gather | bytes 479232 | tf_op jit(solution)/shard_map/all_gather | solution.py:135
  432.1 0.4 multiply_reduce_fusion
  432.5 0.8 multiply_convert_fusion
  433.4 0.0 reduce-scatter.6.cloned.1.call-start
  433.4 0.1 iota_compare_fusion
  433.6 8.0 %all_gather.52 = bf16[1664,208]{1,0:T(8,128)(2,1)S(1)} all-gather(bf16[416,208]{1,0:T(8,128)(2,1)S(1)} %copy-done.5), channel_id=1, replica_groups=mesh['gx'=4,'gy'=8] {'gx'}, dimensions={0}, use_global_device_ids=true | all-gather | bytes 865280 | tf_op jit(solution)/shard_map/all_gather | solution.py:24
  441.6 41.5 %all-gather.24.cloned.1.call-done = bf16[640,1664]{1,0:T(8,128)(2,1)} async-done(((bf16[80,1664]{1,0:T(8,128)(2,1)}), bf16[640,1664]{1,0:T(8,128)(2,1)}) %all-gather.24.cloned.1.call-update) | async-done | bytes 2129936 | tf_op jit(solution)/shard_map/all_gather | solution.py:34
  483.1 4.2 convolution_convert_fusion.5
  487.3 3.1 fusion.202
  490.4 2.4 fusion.81
  492.8 2.3 convolution_convert_fusion.1
  495.1 0.0 all-gather.30.cloned.1.call-start
  495.1 0.5 all-gather.30.cloned.1.call-update
  495.7 0.7 all-gather.32.cloned.1.call-update
  496.5 64.8 %reduce-scatter.6.cloned.1.call-done = bf16[80,1664]{1,0:T(8,128)(2,1)} async-done(((bf16[640,1664]{1,0:T(8,128)(2,1)}), bf16[80,1664]{1,0:T(8,128)(2,1)}) %reduce-scatter.6.cloned.1.call-update) | async-done | bytes 266256 | tf_op jit(solution)/shard_map/reduce_scatter | solution.py:44
  561.2 1.1 fusion.115
  562.4 0.8 fusion.117
  563.3 0.3 reduce-scatter.8.cloned.1.call-start
  563.6 28.4 %all-gather.30.cloned.1.call-done = bf16[1664,1024]{1,0:T(8,128)(2,1)} async-done(((bf16[416,1024]{1,0:T(8,128)(2,1)}), bf16[1664,1024]{1,0:T(8,128)(2,1)}) %all-gather.30.cloned.1.call-update) | async-done | bytes 3407888 | tf_op jit(solution)/shard_map/all_gather | solution.py:24
  591.9 31.7 %all-gather.32.cloned.1.call-done = bf16[1664,1024]{1,0:T(8,128)(2,1)} async-done(((bf16[416,1024]{1,0:T(8,128)(2,1)}), bf16[1664,1024]{1,0:T(8,128)(2,1)}) %all-gather.32.cloned.1.call-update) | async-done | bytes 3407888 | tf_op jit(solution)/shard_map/all_gather | solution.py:24
  623.6 52.1 %all-gather.28.cloned.1.call-done = bf16[640,1664]{1,0:T(8,128)(2,1)} async-done(((bf16[80,1664]{1,0:T(8,128)(2,1)}), bf16[640,1664]{1,0:T(8,128)(2,1)}) %all-gather.28.cloned.1.call-update) | async-done | bytes 2129936 | tf_op jit(solution)/shard_map/all_gather | solution.py:34
  675.7 14.8 %convolution_convert_fusion = bf16[640,1664]{1,0:T(8,128)(2,1)} fusion(bf16[1664,1024]{1,0:T(8,128)(2,1)} %all-gather.32.cloned.1.call-done, bf16[640,1664]{1,0:T(8,128)(2,1)} %all-gather.28.cloned.1.call-done, bf16[1664,1024]{1,0:T(8,128)(2,1)} %all-gather.30.cloned.1.call-done), kind=kOutput, calls=%fused_computation.22 | convolution fusion | flops 4405739520 | bytes 11075584 | tf_op jit(solution)/shard_map/dot_general | solution.py:40
  690.6 66.0 %reduce-scatter.8.cloned.1.call-done = bf16[80,1664]{1,0:T(8,128)(2,1)} async-done(((bf16[640,1664]{1,0:T(8,128)(2,1)}), bf16[80,1664]{1,0:T(8,128)(2,1)}) %reduce-scatter.8.cloned.1.call-update) | async-done | bytes 266256 | tf_op jit(solution)/shard_map/reduce_scatter | solution.py:44
  756.5 1.7 fusion.118
  (39 shorter events, 0.5 us)
Async XLA Ops:
  6.5 7.0 copy-start.4
  6.5 53.3 %all-gather.12.cloned.1.call-start = ((), (), s32[]{:S(2)}) async-start(), calls=%async_computation.3 | async-start | bytes 1916928 | tf_op jit(solution)/shard_map/all_gather | solution.py:34
  11.7 71.4 %all-gather.14.cloned.1.call-start = ((), (), s32[]{:S(2)}) async-start(), calls=%async_computation.4 | async-start | bytes 2662400 | tf_op jit(solution)/shard_map/all_gather | solution.py:24
  12.4 144.4 %reduce-scatter.4.cloned.1.call-start = ((), (), s32[]{:S(2)}) async-start(), calls=%async_computation.5 | async-start | bytes 1916928 | tf_op jit(solution)/shard_map/reduce_scatter | solution.py:44
  88.9 67.9 %copy-start.2 = (bf16[64,1664]{1,0:T(8,128)(2,1)S(1)}, bf16[64,1664]{1,0:T(8,128)(2,1)}, u32[]{:S(2)}) copy-start(bf16[64,1664]{1,0:T(8,128)(2,1)} %param.14) | copy-start | bytes 638980
  90.8 112.5 %all-gather.16.cloned.1.call-start = ((), (), s32[]{:S(2)}) async-start(), calls=%async_computation.6 | async-start | bytes 1916928 | tf_op jit(solution)/shard_map/all_gather | solution.py:34
  158.5 75.3 %all-gather.18.cloned.1.call-start = ((), (), s32[]{:S(2)}) async-start(), calls=%async_computation.7 | async-start | bytes 4259840 | tf_op jit(solution)/shard_map/all_gather | solution.py:24
  159.1 106.2 %all-gather.20.cloned.1.call-start = ((), (), s32[]{:S(2)}) async-start(), calls=%async_computation.8 | async-start | bytes 4259840 | tf_op jit(solution)/shard_map/all_gather | solution.py:24
  159.7 210.8 %all-reduce.2.cloned.1.call-start = ((), (), s32[]{:S(2)}) async-start(), calls=%async_computation.9 | async-start | bytes 3407872 | tf_op jit(solution)/shard_map/psum | solution.py:127
  203.3 2.0 copy-start
  277.9 1.8 copy-start.6
  277.9 120.1 %all-gather.22.cloned.1.call-start = ((), (), s32[]{:S(2)}) async-start(), calls=%async_computation.10 | async-start | bytes 3461120 | tf_op jit(solution)/shard_map/all_gather | solution.py:24
  278.7 162.9 %all-gather.26.cloned.1.call-start = ((), (), s32[]{:S(2)}) async-start(), calls=%async_computation.12 | async-start | bytes 2662400 | tf_op jit(solution)/shard_map/all_gather | solution.py:24
  279.4 203.7 %all-gather.24.cloned.1.call-start = ((), (), s32[]{:S(2)}) async-start(), calls=%async_computation.11 | async-start | bytes 2396160 | tf_op jit(solution)/shard_map/all_gather | solution.py:34
  370.5 2.1 copy-start.1
  375.4 56.7 %copy-start.3 = (bf16[80,1664]{1,0:T(8,128)(2,1)S(1)}, bf16[80,1664]{1,0:T(8,128)(2,1)}, u32[]{:S(2)}) copy-start(bf16[80,1664]{1,0:T(8,128)(2,1)} %param.15) | copy-start | bytes 798724
  400.7 32.9 %copy-start.5 = (bf16[416,208]{1,0:T(8,128)(2,1)S(1)}, bf16[416,208]{1,0:T(8,128)(2,1)}, u32[]{:S(2)}) copy-start(bf16[416,208]{1,0:T(8,128)(2,1)} %param.25) | copy-start | bytes 519172
  433.4 127.9 %reduce-scatter.6.cloned.1.call-start = ((), (), s32[]{:S(2)}) async-start(), calls=%async_computation.13 | async-start | bytes 2396160 | tf_op jit(solution)/shard_map/reduce_scatter | solution.py:44
  495.1 96.8 %all-gather.30.cloned.1.call-start = ((), (), s32[]{:S(2)}) async-start(), calls=%async_computation.15 | async-start | bytes 4259840 | tf_op jit(solution)/shard_map/all_gather | solution.py:24
  495.7 128.0 %all-gather.32.cloned.1.call-start = ((), (), s32[]{:S(2)}) async-start(), calls=%async_computation.16 | async-start | bytes 4259840 | tf_op jit(solution)/shard_map/all_gather | solution.py:24
  496.4 179.3 %all-gather.28.cloned.1.call-start = ((), (), s32[]{:S(2)}) async-start(), calls=%async_computation.14 | async-start | bytes 2396160 | tf_op jit(solution)/shard_map/all_gather | solution.py:34
  563.3 193.3 %reduce-scatter.8.cloned.1.call-start = ((), (), s32[]{:S(2)}) async-start(), calls=%async_computation.17 | async-start | bytes 2396160 | tf_op jit(solution)/shard_map/reduce_scatter | solution.py:44
Sparse Core Ops, SparseCore 0:
  11.8 47.9 all-gather.11
  61.4 21.7 all-gather.13
  90.9 65.8 reduce-scatter.3
  159.1 44.1 all-gather.15
  204.8 28.9 all-gather.17
  235.3 30.0 all-gather.19
  278.1 92.3 all-reduce.1
  372.1 25.8 all-gather.21
  399.6 22.7 all-gather.25
  433.5 49.5 all-gather.23
  495.2 65.9 reduce-scatter.5
  562.7 29.1 all-gather.29
  593.6 30.0 all-gather.31
  625.9 49.7 all-gather.27
  690.7 65.7 reduce-scatter.7
where the time goes:
time: 765 us
  waiting for transfers between devices  630 us (82%)
  matrix products  50.1 us (7%)
  blocking collectives  49.9 us (7%)
  other arithmetic  16.9 us (2%)
  between operations  13.5 us (2%)
    reduce_scatter x3, waiting for transfers between devices, summed_rows(): lax.psum_scatter(term(jnp.int32(0), local_rows * lax.axis_size('gy')).ast...  197 us
    all_gather x4, waiting for transfers between devices, spread_rows(): return project(lax.all_gather(rows, 'gy', axis=0, tiled=True))  173 us
    all_gather x7, waiting for transfers between devices, weight_block(): return lax.all_gather(weight, 'gx', axis=0, tiled=True)  165 us
    psum x1, waiting for transfers between devices, shards(): lax.psum(term.astype(jnp.bfloat16), 'gy').astype(jnp.float32)  90.6 us
    all_gather x1, blocking collectives, shards(): merged_all = lax.all_gather(merged, 'gy', axis=1, tiled=True)  31.4 us
    dot_general x3, matrix products, term(): lax.dot_general(hidden, weight, (((1,), (1,)), ((), ())), preferred_eleme...  19 us
    all_gather x2, blocking collectives, weight_block(): return lax.all_gather(weight, 'gx', axis=0, tiled=True)  18.5 us
  transfers between devices with their start and end apart: 15, of which 14 were waited for; matrix products, arithmetic and copies ran while one was open for 2% of the time, Pallas kernels for 0%

commit v1 on v0

v1 whole, which is shorter than its diff:
```python
import math

import jax
import jax.numpy as jnp
from jax import lax
from jax.sharding import PartitionSpec as P

HEAD_DIM = 104
BF = jnp.bfloat16
F32 = jnp.float32


def layer_norm(rows, gain):
    values = rows.astype(F32)
    center = values - jnp.mean(values, axis=-1, keepdims=True)
    spread = jnp.mean(center * center, axis=-1, keepdims=True)
    return center * lax.rsqrt(spread + 1e-06) * gain


def rms_norm(rows, gain):
    values = rows.astype(F32)
    return values * lax.rsqrt(jnp.mean(values * values, axis=-1, keepdims=True) + 1e-06) * gain


def grid_of(count):
    fast = 2 ** ((count.bit_length() - 1) // 2)
    return count // fast, fast


def moved(value, dz, dx):
    nz, nx = grid_of(lax.axis_size("gy"))
    pairs = [
        (z * nx + x, ((z + dz) % nz) * nx + (x + dx) % nx) for z in range(nz) for x in range(nx)
    ]
    return lax.ppermute(value, "gy", pairs)


def far_first(nz):
    return sorted(range(1, nz), key=lambda k: -min(k, nz - k))


def relative_blocks(value):
    nz, nx = grid_of(lax.axis_size("gy"))
    found = {(0, 0): value}
    for k in far_first(nz):
        found[k, 0] = moved(value, -k, 0)
    for k in [0] + sorted(range(1, nz), key=lambda k: min(k, nz - k)):
        for p in range(1, nx):
            found[k, p] = moved(found[k, 0], 0, -p)
    return [found[k, p] for k in range(nz) for p in range(nx)]


def relative_gather(value):
    return jnp.concatenate(relative_blocks(value), axis=0)


def relative_owner():
    nz, nx = grid_of(lax.axis_size("gy"))
    me = lax.axis_index("gy")
    z, x = me // nx, me % nx
    return jnp.stack([((z + k) % nz) * nx + (x + p) % nx for k in range(nz) for p in range(nx)])


def relative_scatter(term, local):
    nz, nx = grid_of(lax.axis_size("gy"))
    pieces = {
        (k, p): term[(k * nx + p) * local : (k * nx + p + 1) * local]
        for k in range(nz)
        for p in range(nx)
    }
    sums = {}
    for k in far_first(nz) + [0]:
        total = pieces[k, 0].astype(F32)
        for p in range(1, nx):
            total = total + moved(pieces[k, p], 0, p).astype(F32)
        sums[k] = total
    out = sums[0]
    for k in far_first(nz):
        out = out + moved(sums[k].astype(BF), k, 0).astype(F32)
    return out


def absolute_rows(value):
    nz, nx = grid_of(lax.axis_size("gy"))
    me = lax.axis_index("gy")
    z, x = me // nx, me % nx
    blocks = value.reshape(nz, nx, value.shape[0] // (nz * nx), value.shape[1])
    blocks = lax.dynamic_slice_in_dim(jnp.concatenate([blocks] * 2, 0), (nz - z) % nz, nz, 0)
    blocks = lax.dynamic_slice_in_dim(jnp.concatenate([blocks] * 2, 1), (nx - x) % nx, nx, 1)
    return blocks.reshape(value.shape)


def small_weight(weight):
    count = lax.axis_size("gx")
    me = lax.axis_index("gx")
    rows = weight.shape[0]
    whole = jnp.zeros((rows * count, weight.shape[1]), weight.dtype)
    for j in range(count // 2):
        along = weight
        if j:
            along = lax.ppermute(weight, "gx", [(i, (i - 2 * j) % count) for i in range(count)])
        other = lax.ppermute(along, "gx", [(i, i ^ 1) for i in range(count)])
        spot = (me + 2 * j) % count
        whole = lax.dynamic_update_slice(whole, along, (spot * rows, 0))
        whole = lax.dynamic_update_slice(whole, other, ((spot ^ 1) * rows, 0))
    return whole


def weight_block(weight):
    return lax.all_gather(weight, "gx", axis=0, tiled=True)


def tied(first, *later):
    return lax.optimization_barrier((first, *later))


def attend(joined, allowed):
    total = joined.shape[0]
    heads_here = joined.shape[1] // (3 * HEAD_DIM)
    grouped = joined.reshape(total, heads_here, 3, HEAD_DIM)
    query = grouped[:, :, 0]
    keys = grouped[:, :, 1]
    values = grouped[:, :, 2]
    scale = 1.0 / math.sqrt(HEAD_DIM)
    scores = jnp.einsum("qhe,khe->hqk", query, keys, preferred_element_type=F32) * scale
    scores = jnp.where(allowed[None], scores, -1e30)
    top = jnp.max(scores, axis=-1, keepdims=True)
    weights = jnp.exp(scores - top)
    probs = (weights / jnp.sum(weights, axis=-1, keepdims=True)).astype(BF)
    mixed = jnp.einsum("hqk,khe->qhe", probs, values, preferred_element_type=F32)
    return mixed.astype(BF).reshape(total, heads_here * HEAD_DIM)


def out_term(hidden, weight):
    return lax.dot_general(
        hidden, weight, (((1,), (1,)), ((), ())), preferred_element_type=F32
    ).astype(BF)


def shards(
    patches,
    prompt,
    image_ids,
    positions,
    norm_gains,
    vit_qkv,
    vit_out,
    vit_up,
    vit_down,
    merge_proj,
    dec_qkv,
    dec_out,
    dec_up,
    dec_down,
):
    local = patches.shape[0]
    width = patches.shape[1]
    seq_local = prompt.shape[0]
    owner = relative_owner()
    rows_of = (owner[:, None] * local + jnp.arange(local, dtype=jnp.int32)).reshape(-1)
    spots_of = (owner[:, None] * seq_local + jnp.arange(seq_local, dtype=jnp.int32)).reshape(-1)
    labels = image_ids[0][rows_of // 4]

    qkv_block = weight_block(vit_qkv)
    enc_in = relative_gather(layer_norm(patches, norm_gains[0]).astype(BF))
    enc_qkv = jnp.dot(enc_in, qkv_block, preferred_element_type=F32).astype(BF)
    out_block = small_weight(vit_out)
    enc_qkv, out_block, vit_up = tied(enc_qkv, out_block, vit_up)
    enc_mix = attend(enc_qkv, labels[:, None] == labels[None, :])
    summed = relative_scatter(out_term(enc_mix, out_block), local)
    enc_mid = (patches.astype(F32) + summed).astype(BF)
    up_block = weight_block(vit_up)
    enc_mid, up_block, vit_down = tied(enc_mid, up_block, vit_down)

    down_block = weight_block(vit_down)
    normed = relative_gather(layer_norm(enc_mid, norm_gains[1]).astype(BF))
    normed, down_block, merge_proj, prompt = tied(normed, down_block, merge_proj, prompt)
    merge_block = weight_block(merge_proj)
    hidden = jax.nn.gelu(
        jnp.dot(normed, up_block, preferred_element_type=F32), approximate=False
    ).astype(BF)
    summed = relative_scatter(out_term(hidden, down_block), local)
    enc_out = (enc_mid.astype(F32) + summed).astype(BF)
    enc_out, merge_block, dec_qkv = tied(enc_out, merge_block, dec_qkv)

    dqkv_block = weight_block(dec_qkv)
    windows = layer_norm(enc_out, norm_gains[2]).astype(BF).reshape(local // 4, 4 * width)
    windows = relative_gather(windows)
    prompt_all = relative_gather(prompt)
    merged = jnp.dot(windows, merge_block, preferred_element_type=F32).astype(BF)
    merged, dqkv_block, dec_up = tied(merged, dqkv_block, dec_up)
    merged_all = lax.all_gather(absolute_rows(merged), "gy", axis=1, tiled=True)
    hits = positions[0][None, :] == spots_of[:, None]
    placed = jnp.dot(hits.astype(BF), merged_all, preferred_element_type=F32).astype(BF)
    dec_all = jnp.where(jnp.any(hits, axis=1)[:, None], placed, prompt_all)
    dec_in = dec_all[:seq_local]

    dup_block = weight_block(dec_up)
    dout_block = small_weight(dec_out)
    dnormed = rms_norm(dec_all, norm_gains[3]).astype(BF)
    dec_rows = jnp.dot(dnormed, dqkv_block, preferred_element_type=F32).astype(BF)
    dec_mix = attend(dec_rows, spots_of[:, None] >= spots_of[None, :])
    summed = relative_scatter(out_term(dec_mix, dout_block), seq_local)
    dec_mid = (dec_in.astype(F32) + summed).astype(BF)
    dec_mid, dup_block, dec_down = tied(dec_mid, dup_block, dec_down)

    ddown_block = weight_block(dec_down)
    enormed = relative_gather(rms_norm(dec_mid, norm_gains[4]).astype(BF))
    dec_hidden = jax.nn.gelu(
        jnp.dot(enormed, dup_block, preferred_element_type=F32), approximate=False
    ).astype(BF)
    summed = relative_scatter(out_term(dec_hidden, ddown_block), seq_local)
    return (dec_mid.astype(F32) + summed).astype(BF)


def solution(mesh):
    weight = P("gx", "gy")
    rows = P(("gx", "gy"), None)
    in_specs = (rows, rows, P("gx", None), P("gx", None), P()) + (weight,) * 9
    return jax.shard_map(shards, mesh=mesh, in_specs=in_specs, out_specs=rows, check_vma=False)
```

time: 765 us -> 414 us (0.54)
  waiting for transfers between devices: 630 us -> 201 us
  starting transfers between devices: 1.22 us -> 68.5 us
  local copies, waits for them, and re-layouts: 3.25 us -> 35.2 us
  blocking collectives: 49.9 us -> 31.4 us
    ppermute x0 -> x69, waiting for transfers between devices: none -> 198 us  [the longest x63 192 us: moved(): return lax.ppermute(value, 'gy', pairs)]
    reduce_scatter x3 -> x0, waiting for transfers between devices: 197 us -> none  [summed_rows(): lax.psum_scatter(term(jnp.int32(0), local_rows * lax.axis_size('gy')).ast...]
    all_gather x4 -> x0, waiting for transfers between devices: 173 us -> none  [spread_rows(): return project(lax.all_gather(rows, 'gy', axis=0, tiled=True))]
    all_gather x7, waiting for transfers between devices: 165 us -> 3.04 us  [weight_block(): return lax.all_gather(weight, 'gx', axis=0, tiled=True)]
    psum x1 -> x0, waiting for transfers between devices: 90.6 us -> none  [shards(): lax.psum(term.astype(jnp.bfloat16), 'gy').astype(jnp.float32)]
    ppermute x0 -> x69, starting transfers between devices: none -> 68.1 us  [the longest x63 64.6 us: moved(): return lax.ppermute(value, 'gy', pairs)]
    unnamed x14 -> x50, local copies, waits for them, and re-layouts: 0.11 us -> 25.7 us
    all_gather x3 -> x1, blocking collectives: 49.9 us -> 31.4 us  [shards(): merged_all = lax.all_gather(absolute_rows(merged), 'gy', axis=1, tiled=True)]
  transfers between devices with their start and end apart: 15 -> 76, of which waited for: 14 -> 44; matrix products, arithmetic and copies ran while one was open for 2% -> 18% of each run, Pallas kernels for 0% -> 0%
where the time goes in v1:
time: 414 us; the launch traced here: 406 us
  waiting for transfers between devices  201 us (49%)
  starting transfers between devices  68.5 us (17%)
  matrix products  43.9 us (11%)
  local copies, waits for them, and re-layouts  35.2 us (9%)
  blocking collectives  31.4 us (8%)
  between operations  14.6 us (4%)
  other arithmetic  11.1 us (3%)
    ppermute x63, waiting for transfers between devices, moved(): return lax.ppermute(value, 'gy', pairs)  192 us
    ppermute x63, starting transfers between devices, moved(): return lax.ppermute(value, 'gy', pairs)  64.6 us
    all_gather x1, blocking collectives, shards(): merged_all = lax.all_gather(absolute_rows(merged), 'gy', axis=1, tiled=True)  31.4 us
    dot_general x4, matrix products, out_term(): lax.dot_general(hidden, weight, (((1,), (1,)), ((), ())), preferred_eleme...  26.8 us
    unnamed x50, local copies, waits for them, and re-layouts  25.7 us
  transfers between devices with their start and end apart: 76, of which 44 were waited for; matrix products, arithmetic and copies ran while one was open for 18% of the time, Pallas kernels for 0%

profile of v1, /device:TPU:0, one launch (start us, length us, event | category | flops | bytes accessed | tf_op | source)
XLA Modules:
  0.0 406.2 jit_solution(10895851756386493396)
XLA Ops:
  7.0 2.6 collective-permute-start.8
  13.0 1.8 constant_dynamic-update-slice_fusion.7
  16.3 3.6 collective-permute-start.1
  21.1 4.5 %collective-permute-done.1 = bf16[64,1664]{1,0:T(8,128)(2,1)S(1)} collective-permute-done((bf16[64,1664]{1,0:T(8,128)(2,1)S(1)}, bf16[64,1664]{1,0:T(8,128)(2,1)S(1)}, u32[]{:S(2)}, u32[]{:S(2)}) %collective-permute-start.1) | collective-permute-done | bytes 213024 | tf_op jit(solution)/shard_map/ppermute | solution.py:35
  27.5 10.5 %collective-permute-done.3 = bf16[64,1664]{1,0:T(8,128)(2,1)S(1)} collective-permute-done((bf16[64,1664]{1,0:T(8,128)(2,1)S(1)}, bf16[64,1664]{1,0:T(8,128)(2,1)S(1)}, u32[]{:S(2)}, u32[]{:S(2)}) %collective-permute-start.3) | collective-permute-done | bytes 213024 | tf_op jit(solution)/shard_map/ppermute | solution.py:35
  41.5 4.7 %collective-permute-done.4 = bf16[64,1664]{1,0:T(8,128)(2,1)S(1)} collective-permute-done((bf16[64,1664]{1,0:T(8,128)(2,1)S(1)}, bf16[64,1664]{1,0:T(8,128)(2,1)S(1)}, u32[]{:S(2)}, u32[]{:S(2)}) %collective-permute-start.4) | collective-permute-done | bytes 213024 | tf_op jit(solution)/shard_map/ppermute | solution.py:35
  49.5 3.5 convolution_convert_fusion.5
  53.4 3.3 gather_fusion
  64.2 4.1 %collective-permute-done.11 = bf16[64,1664]{1,0:T(8,128)(2,1)S(1)} collective-permute-done((bf16[64,1664]{1,0:T(8,128)(2,1)S(1)}, bf16[64,1664]{1,0:T(8,128)(2,1)S(1)}, u32[]{:S(2)}, u32[]{:S(2)}) %collective-permute-start.11) | collective-permute-done | bytes 213024 | tf_op jit(solution)/shard_map/ppermute | solution.py:35
  68.3 4.6 %collective-permute-done.15 = bf16[64,1664]{1,0:T(8,128)(2,1)S(1)} collective-permute-done((bf16[64,1664]{1,0:T(8,128)(2,1)S(1)}, bf16[64,1664]{1,0:T(8,128)(2,1)S(1)}, u32[]{:S(2)}, u32[]{:S(2)}) %collective-permute-start.15) | collective-permute-done | bytes 213024 | tf_op jit(solution)/shard_map/ppermute | solution.py:35
  72.9 3.9 collective-permute-done.13
  77.0 2.0 collective-permute-start.14
  79.3 4.4 %collective-permute-done.16 = bf16[64,1664]{1,0:T(8,128)(2,1)S(1)} collective-permute-done((bf16[64,1664]{1,0:T(8,128)(2,1)S(1)}, bf16[64,1664]{1,0:T(8,128)(2,1)S(1)}, u32[]{:S(2)}, u32[]{:S(2)}) %collective-permute-start.16) | collective-permute-done | bytes 213024 | tf_op jit(solution)/shard_map/ppermute | solution.py:35
  83.6 3.5 collective-permute-done.14
  87.1 5.8 %collective-permute-done.12 = bf16[64,1664]{1,0:T(8,128)(2,1)S(1)} collective-permute-done((bf16[64,1664]{1,0:T(8,128)(2,1)S(1)}, bf16[64,1664]{1,0:T(8,128)(2,1)S(1)}, u32[]{:S(2)}, u32[]{:S(2)}) %collective-permute-start.12) | collective-permute-done | bytes 213024 | tf_op jit(solution)/shard_map/ppermute | solution.py:35
  94.6 6.3 %collective-permute-done.46 = bf16[416,208]{1,0:T(8,128)(2,1)S(1)} collective-permute-done((bf16[416,208]{1,0:T(8,128)(2,1)S(1)}, bf16[416,208]{1,0:T(8,128)(2,1)S(1)}, u32[]{:S(2)}, u32[]{:S(2)}) %collective-permute-start.46) | collective-permute-done | bytes 173088 | tf_op jit(solution)/shard_map/ppermute | solution.py:101
  102.8 2.0 collective-permute-start.18
  105.4 6.4 %collective-permute-done.18 = bf16[64,1664]{1,0:T(8,128)(2,1)S(1)} collective-permute-done((bf16[64,1664]{1,0:T(8,128)(2,1)S(1)}, bf16[64,1664]{1,0:T(8,128)(2,1)S(1)}, u32[]{:S(2)}, u32[]{:S(2)}) %collective-permute-start.18) | collective-permute-done | bytes 213024 | tf_op jit(solution)/shard_map/ppermute | solution.py:35
  113.4 9.2 %collective-permute-done.20 = bf16[64,1664]{1,0:T(8,128)(2,1)S(1)} collective-permute-done((bf16[64,1664]{1,0:T(8,128)(2,1)S(1)}, bf16[64,1664]{1,0:T(8,128)(2,1)S(1)}, u32[]{:S(2)}, u32[]{:S(2)}) %collective-permute-start.20) | collective-permute-done | bytes 213024 | tf_op jit(solution)/shard_map/ppermute | solution.py:35
  127.4 3.3 collective-permute-done.21
  132.1 1.8 collective-permute-done.23
  136.3 11.8 %convolution_convert_fusion.3 = bf16[512,1664]{1,0:T(8,128)(2,1)S(1)} fusion(bf16[1664,1024]{1,0:T(8,128)(2,1)} %all-gather.12.cloned.1.call-done, bf16[512,1664]{1,0:T(8,128)(2,1)} %constant_dynamic-update-slice_fusion.8, bf16[1664,1024]{1,0:T(8,128)(2,1)} %all-gather.10.cloned.1.call-done), kind=kOutput, calls=%fused_computation.16 | convolution fusion | flops 3524591616 | bytes 10223616 | tf_op jit(solution)/shard_map/dot_general | solution.py:135
  150.8 1.7 constant_dynamic-update-slice_fusion.31
  152.5 3.9 collective-permute-done.25
  156.4 4.2 %collective-permute-done.29 = bf16[64,1664]{1,0:T(8,128)(2,1)S(1)} collective-permute-done((bf16[64,1664]{1,0:T(8,128)(2,1)S(1)}, bf16[64,1664]{1,0:T(8,128)(2,1)S(1)}, u32[]{:S(2)}, u32[]{:S(2)}) %collective-permute-start.29) | collective-permute-done | bytes 213024 | tf_op jit(solution)/shard_map/ppermute | solution.py:35
  160.6 1.7 collective-permute-start.43
  165.3 1.7 constant_dynamic-update-slice_fusion.30
  166.9 1.8 collective-permute-done.24
  168.8 1.9 collective-permute-start.28
  170.9 1.7 constant_dynamic-update-slice_fusion.29
  172.5 11.7 %collective-permute-done.41 = bf16[80,1664]{1,0:T(8,128)(2,1)} collective-permute-done((bf16[80,1664]{1,0:T(8,128)(2,1)}, bf16[80,1664]{1,0:T(8,128)(2,1)}, u32[]{:S(2)}, u32[]{:S(2)}) %collective-permute-start.41) | collective-permute-done | bytes 266272 | tf_op jit(solution)/shard_map/ppermute | solution.py:35
  186.8 4.0 collective-permute-done.26
  191.7 1.7 constant_dynamic-update-slice_fusion.27
  196.2 5.1 %collective-permute-done.31 = bf16[16,6656]{1,0:T(8,128)(2,1)} collective-permute-done((bf16[16,6656]{1,0:T(8,128)(2,1)S(1)}, bf16[16,6656]{1,0:T(8,128)(2,1)}, u32[]{:S(2)}, u32[]{:S(2)}) %collective-permute-start.31) | collective-permute-done | bytes 213024 | tf_op jit(solution)/shard_map/ppermute | solution.py:35
  205.3 6.8 %collective-permute-done.34 = bf16[16,6656]{1,0:T(8,128)(2,1)S(1)} collective-permute-done((bf16[16,6656]{1,0:T(8,128)(2,1)S(1)}, bf16[16,6656]{1,0:T(8,128)(2,1)S(1)}, u32[]{:S(2)}, u32[]{:S(2)}) %collective-permute-start.34) | collective-permute-done | bytes 213024 | tf_op jit(solution)/shard_map/ppermute | solution.py:35
  214.2 4.3 %collective-permute-done.35 = bf16[16,6656]{1,0:T(8,128)(2,1)S(1)} collective-permute-done((bf16[16,6656]{1,0:T(8,128)(2,1)S(1)}, bf16[16,6656]{1,0:T(8,128)(2,1)S(1)}, u32[]{:S(2)}, u32[]{:S(2)}) %collective-permute-start.35) | collective-permute-done | bytes 213024 | tf_op jit(solution)/shard_map/ppermute | solution.py:35
  218.5 2.2 collective-permute-done.37
  221.8 1.7 constant_dynamic-update-slice_fusion.26
  223.4 1.7 constant_dynamic-update-slice_fusion.25
  225.1 1.7 constant_dynamic-update-slice_fusion.24
  227.1 31.4 %all_gather.29 = bf16[128,1664]{0,1:T(8,128)(2,1)S(1)} all-gather(bf16[128,208]{0,1:T(8,128)(2,1)S(1)} %copy.47), channel_id=1, replica_groups=mesh['gx'=4,'gy'=8] {'gy'}, dimensions={1}, use_global_device_ids=true | all-gather | bytes 479232 | tf_op jit(solution)/shard_map/all_gather | solution.py:192
  258.6 2.8 fusion.2
  261.4 2.2 fusion.36
  263.6 3.2 fusion.212
  266.7 2.4 fusion.70
  270.1 2.0 collective-permute-start.53
  272.2 1.9 collective-permute-start.48
  274.2 4.1 %collective-permute-done.49 = bf16[80,1664]{1,0:T(8,128)(2,1)S(1)} collective-permute-done((bf16[80,1664]{1,0:T(8,128)(2,1)S(1)}, bf16[80,1664]{1,0:T(8,128)(2,1)S(1)}, u32[]{:S(2)}, u32[]{:S(2)}) %collective-permute-start.49) | collective-permute-done | bytes 266272 | tf_op jit(solution)/shard_map/ppermute | solution.py:35
  278.3 2.9 collective-permute-done.53
  281.2 2.9 collective-permute-done.51
  284.2 2.6 collective-permute-start.54
  287.5 7.7 %collective-permute-done.54 = bf16[80,1664]{1,0:T(8,128)(2,1)S(1)} collective-permute-done((bf16[80,1664]{1,0:T(8,128)(2,1)S(1)}, bf16[80,1664]{1,0:T(8,128)(2,1)S(1)}, u32[]{:S(2)}, u32[]{:S(2)}) %collective-permute-start.54) | collective-permute-done | bytes 266272 | tf_op jit(solution)/shard_map/ppermute | solution.py:35
  296.4 11.0 %collective-permute-done.50 = bf16[80,1664]{1,0:T(8,128)(2,1)S(1)} collective-permute-done((bf16[80,1664]{1,0:T(8,128)(2,1)S(1)}, bf16[80,1664]{1,0:T(8,128)(2,1)S(1)}, u32[]{:S(2)}, u32[]{:S(2)}) %collective-permute-start.50) | collective-permute-done | bytes 266272 | tf_op jit(solution)/shard_map/ppermute | solution.py:35
  309.7 2.7 collective-permute-start.56
  317.9 7.4 %collective-permute-done.58 = bf16[80,1664]{1,0:T(8,128)(2,1)S(1)} collective-permute-done((bf16[80,1664]{1,0:T(8,128)(2,1)S(1)}, bf16[80,1664]{1,0:T(8,128)(2,1)S(1)}, u32[]{:S(2)}, u32[]{:S(2)}) %collective-permute-start.58) | collective-permute-done | bytes 266272 | tf_op jit(solution)/shard_map/ppermute | solution.py:35
  335.4 3.0 all-gather.20.cloned.1.call-done
  338.3 13.4 %convolution_convert_fusion.1 = bf16[640,1664]{1,0:T(8,128)(2,1)S(1)} fusion(bf16[1664,1024]{1,0:T(8,128)(2,1)} %all-gather.20.cloned.1.call-done, bf16[640,1664]{1,0:T(8,128)(2,1)} %constant_dynamic-update-slice_fusion.32, bf16[1664,1024]{1,0:T(8,128)(2,1)} %all-gather.18.cloned.1.call-done), kind=kOutput, calls=%fused_computation.13 | convolution fusion | flops 4405739520 | bytes 11075584 | tf_op jit(solution)/shard_map/dot_general | solution.py:135
  356.0 5.2 %collective-permute-done.63 = bf16[80,1664]{1,0:T(8,128)(2,1)S(1)} collective-permute-done((bf16[80,1664]{1,0:T(8,128)(2,1)S(1)}, bf16[80,1664]{1,0:T(8,128)(2,1)S(1)}, u32[]{:S(2)}, u32[]{:S(2)}) %collective-permute-start.63) | collective-permute-done | bytes 266272 | tf_op jit(solution)/shard_map/ppermute | solution.py:35
  361.1 5.7 %collective-permute-done.67 = bf16[80,1664]{1,0:T(8,128)(2,1)S(1)} collective-permute-done((bf16[80,1664]{1,0:T(8,128)(2,1)S(1)}, bf16[80,1664]{1,0:T(8,128)(2,1)S(1)}, u32[]{:S(2)}, u32[]{:S(2)}) %collective-permute-start.67) | collective-permute-done | bytes 266272 | tf_op jit(solution)/shard_map/ppermute | solution.py:35
  366.9 5.7 %collective-permute-done.65 = bf16[80,1664]{1,0:T(8,128)(2,1)S(1)} collective-permute-done((bf16[80,1664]{1,0:T(8,128)(2,1)S(1)}, bf16[80,1664]{1,0:T(8,128)(2,1)S(1)}, u32[]{:S(2)}, u32[]{:S(2)}) %collective-permute-start.65) | collective-permute-done | bytes 266272 | tf_op jit(solution)/shard_map/ppermute | solution.py:35
  372.8 3.4 collective-permute-start.68
  377.6 5.5 %collective-permute-done.68 = bf16[80,1664]{1,0:T(8,128)(2,1)S(1)} collective-permute-done((bf16[80,1664]{1,0:T(8,128)(2,1)S(1)}, bf16[80,1664]{1,0:T(8,128)(2,1)S(1)}, u32[]{:S(2)}, u32[]{:S(2)}) %collective-permute-start.68) | collective-permute-done | bytes 266272 | tf_op jit(solution)/shard_map/ppermute | solution.py:35
  383.0 6.8 %collective-permute-done.66 = bf16[80,1664]{1,0:T(8,128)(2,1)S(1)} collective-permute-done((bf16[80,1664]{1,0:T(8,128)(2,1)S(1)}, bf16[80,1664]{1,0:T(8,128)(2,1)S(1)}, u32[]{:S(2)}, u32[]{:S(2)}) %collective-permute-start.66) | collective-permute-done | bytes 266272 | tf_op jit(solution)/shard_map/ppermute | solution.py:35
  389.8 8.1 %collective-permute-done.64 = bf16[80,1664]{1,0:T(8,128)(2,1)S(1)} collective-permute-done((bf16[80,1664]{1,0:T(8,128)(2,1)S(1)}, bf16[80,1664]{1,0:T(8,128)(2,1)S(1)}, u32[]{:S(2)}, u32[]{:S(2)}) %collective-permute-start.64) | collective-permute-done | bytes 266272 | tf_op jit(solution)/shard_map/ppermute | solution.py:35
  (222 shorter events, 84.6 us)
Async XLA Ops:
  6.5 42.9 %all-gather.8.cloned.1.call-start = ((), (), s32[]{:S(2)}) async-start(), calls=%async_computation | async-start | bytes 2662400 | tf_op jit(solution)/shard_map/all_gather | solution.py:110
  6.5 13.4 %collective-permute-start.7 = (bf16[416,208]{1,0:T(8,128)(2,1)}, bf16[416,208]{1,0:T(8,128)(2,1)S(1)}, u32[]{:S(2)}, u32[]{:S(2)}) collective-permute-start(bf16[416,208]{1,0:T(8,128)(2,1)} %param.20), channel_id=1, source_target_pairs={{0,8},{8,0},{16,24},{24,16},{1,9},{9,1},{17,25},{25,17},{2,10},{10... | collective-permute-start | bytes 519176 | tf_op jit(solution)/shard_map/ppermute | solution.py:102
  7.0 14.1 %collective-permute-start.8 = (bf16[416,208]{1,0:T(8,128)(2,1)}, bf16[416,208]{1,0:T(8,128)(2,1)S(1)}, u32[]{:S(2)}, u32[]{:S(2)}) collective-permute-start(bf16[416,208]{1,0:T(8,128)(2,1)} %param.20), channel_id=1, source_target_pairs={{0,16},{8,24},{16,0},{24,8},{1,17},{9,25},{17,1},{25,9},{2,18},{10... | collective-permute-start | bytes 519176 | tf_op jit(solution)/shard_map/ppermute | solution.py:101
  9.6 83.5 %all-gather.10.cloned.1.call-start = ((), (), s32[]{:S(2)}) async-start(), calls=%async_computation.1 | async-start | bytes 4259840 | tf_op jit(solution)/shard_map/all_gather | solution.py:110
  14.8 11.3 %collective-permute-start = (bf16[64,1664]{1,0:T(8,128)(2,1)S(1)}, bf16[64,1664]{1,0:T(8,128)(2,1)S(1)}, u32[]{:S(2)}, u32[]{:S(2)}) collective-permute-start(bf16[64,1664]{1,0:T(8,128)(2,1)S(1)} %get-tuple-element.53), channel_id=1, source_target_pairs={{0,1},{1,0},{2,3},{3,2},{4,5},{5,4},{6,7},{7,6},{8,9},{9,8},{10,11... | collective-permute-start | bytes 638984 | tf_op jit(solution)/shard_map/ppermute | solution.py:35
  16.3 9.3 %collective-permute-start.1 = (bf16[64,1664]{1,0:T(8,128)(2,1)S(1)}, bf16[64,1664]{1,0:T(8,128)(2,1)S(1)}, u32[]{:S(2)}, u32[]{:S(2)}) collective-permute-start(bf16[64,1664]{1,0:T(8,128)(2,1)S(1)} %get-tuple-element.53), channel_id=1, source_target_pairs={{0,6},{1,7},{2,0},{3,1},{4,2},{5,3},{6,4},{7,5},{8,14},{9,15},{10,... | collective-permute-start | bytes 638984 | tf_op jit(solution)/shard_map/ppermute | solution.py:35
  19.9 18.1 %collective-permute-start.3 = (bf16[64,1664]{1,0:T(8,128)(2,1)S(1)}, bf16[64,1664]{1,0:T(8,128)(2,1)S(1)}, u32[]{:S(2)}, u32[]{:S(2)}) collective-permute-start(bf16[64,1664]{1,0:T(8,128)(2,1)S(1)} %get-tuple-element.53), channel_id=1, source_target_pairs={{0,4},{1,5},{2,6},{3,7},{4,0},{5,1},{6,2},{7,3},{8,12},{9,13},{10,... | collective-permute-start | bytes 638984 | tf_op jit(solution)/shard_map/ppermute | solution.py:35
  20.0 18.6 %collective-permute-start.5 = (bf16[64,1664]{1,0:T(8,128)(2,1)S(1)}, bf16[64,1664]{1,0:T(8,128)(2,1)S(1)}, u32[]{:S(2)}, u32[]{:S(2)}) collective-permute-start(bf16[64,1664]{1,0:T(8,128)(2,1)S(1)} %get-tuple-element.53), channel_id=1, source_target_pairs={{0,2},{1,3},{2,4},{3,5},{4,6},{5,7},{6,0},{7,1},{8,10},{9,11},{10,... | collective-permute-start | bytes 638984 | tf_op jit(solution)/shard_map/ppermute | solution.py:35
  21.1 19.0 %collective-permute-start.9 = (bf16[416,208]{1,0:T(8,128)(2,1)S(1)}, bf16[416,208]{1,0:T(8,128)(2,1)S(1)}, u32[]{:S(2)}, u32[]{:S(2)}) collective-permute-start(bf16[416,208]{1,0:T(8,128)(2,1)S(1)} %collective-permute-done.8), channel_id=1, source_target_pairs={{0,8},{8,0},{16,24},{24,16},{1,9},{9,1},{17,25},{25,17},{2,10},{10... | collective-permute-start | bytes 519176 | tf_op jit(solution)/shard_map/ppermute | solution.py:102
  25.6 14.5 %collective-permute-start.2 = (bf16[64,1664]{1,0:T(8,128)(2,1)S(1)}, bf16[64,1664]{1,0:T(8,128)(2,1)S(1)}, u32[]{:S(2)}, u32[]{:S(2)}) collective-permute-start(bf16[64,1664]{1,0:T(8,128)(2,1)S(1)} %collective-permute-done.1), channel_id=1, source_target_pairs={{0,1},{1,0},{2,3},{3,2},{4,5},{5,4},{6,7},{7,6},{8,9},{9,8},{10,11... | collective-permute-start | bytes 638984 | tf_op jit(solution)/shard_map/ppermute | solution.py:35
  38.0 8.2 %collective-permute-start.4 = (bf16[64,1664]{1,0:T(8,128)(2,1)S(1)}, bf16[64,1664]{1,0:T(8,128)(2,1)S(1)}, u32[]{:S(2)}, u32[]{:S(2)}) collective-permute-start(bf16[64,1664]{1,0:T(8,128)(2,1)S(1)} %collective-permute-done.3), channel_id=1, source_target_pairs={{0,1},{1,0},{2,3},{3,2},{4,5},{5,4},{6,7},{7,6},{8,9},{9,8},{10,11... | collective-permute-start | bytes 638984 | tf_op jit(solution)/shard_map/ppermute | solution.py:35
  38.6 10.2 %collective-permute-start.6 = (bf16[64,1664]{1,0:T(8,128)(2,1)S(1)}, bf16[64,1664]{1,0:T(8,128)(2,1)S(1)}, u32[]{:S(2)}, u32[]{:S(2)}) collective-permute-start(bf16[64,1664]{1,0:T(8,128)(2,1)S(1)} %collective-permute-done.5), channel_id=1, source_target_pairs={{0,1},{1,0},{2,3},{3,2},{4,5},{5,4},{6,7},{7,6},{8,9},{9,8},{10,11... | collective-permute-start | bytes 638984 | tf_op jit(solution)/shard_map/ppermute | solution.py:35
  53.0 81.6 %all-gather.12.cloned.1.call-start = ((), (), s32[]{:S(2)}) async-start(), calls=%async_computation.2 | async-start | bytes 4259840 | tf_op jit(solution)/shard_map/all_gather | solution.py:110
  60.1 8.3 %collective-permute-start.11 = (bf16[64,1664]{1,0:T(8,128)(2,1)S(1)}, bf16[64,1664]{1,0:T(8,128)(2,1)S(1)}, u32[]{:S(2)}, u32[]{:S(2)}) collective-permute-start(bf16[64,1664]{1,0:T(8,128)(2,1)S(1)} %get-tuple-element.78), channel_id=1, source_target_pairs={{0,1},{1,0},{2,3},{3,2},{4,5},{5,4},{6,7},{7,6},{8,9},{9,8},{10,11... | collective-permute-start | bytes 638984 | tf_op jit(solution)/shard_map/ppermute | solution.py:35
  60.7 12.2 %collective-permute-start.15 = (bf16[64,1664]{1,0:T(8,128)(2,1)S(1)}, bf16[64,1664]{1,0:T(8,128)(2,1)S(1)}, u32[]{:S(2)}, u32[]{:S(2)}) collective-permute-start(bf16[64,1664]{1,0:T(8,128)(2,1)S(1)} %get-tuple-element.76), channel_id=1, source_target_pairs={{0,1},{1,0},{2,3},{3,2},{4,5},{5,4},{6,7},{7,6},{8,9},{9,8},{10,11... | collective-permute-start | bytes 638984 | tf_op jit(solution)/shard_map/ppermute | solution.py:35
  62.2 14.6 %collective-permute-start.13 = (bf16[64,1664]{1,0:T(8,128)(2,1)S(1)}, bf16[64,1664]{1,0:T(8,128)(2,1)S(1)}, u32[]{:S(2)}, u32[]{:S(2)}) collective-permute-start(bf16[64,1664]{1,0:T(8,128)(2,1)S(1)} %get-tuple-element.77), channel_id=1, source_target_pairs={{0,1},{1,0},{2,3},{3,2},{4,5},{5,4},{6,7},{7,6},{8,9},{9,8},{10,11... | collective-permute-start | bytes 638984 | tf_op jit(solution)/shard_map/ppermute | solution.py:35
  62.7 16.5 %collective-permute-start.10 = (bf16[64,1664]{1,0:T(8,128)(2,1)S(1)}, bf16[64,1664]{1,0:T(8,128)(2,1)S(1)}, u32[]{:S(2)}, u32[]{:S(2)}) collective-permute-start(bf16[64,1664]{1,0:T(8,128)(2,1)S(1)} %get-tuple-element.75), channel_id=1, source_target_pairs={{0,1},{1,0},{2,3},{3,2},{4,5},{5,4},{6,7},{7,6},{8,9},{9,8},{10,11... | collective-permute-start | bytes 638984 | tf_op jit(solution)/shard_map/ppermute | solution.py:35
  77.0 10.1 %collective-permute-start.14 = (bf16[64,1664]{1,0:T(8,128)(2,1)S(1)}, bf16[64,1664]{1,0:T(8,128)(2,1)S(1)}, u32[]{:S(2)}, u32[]{:S(2)}) collective-permute-start(bf16[64,1664]{1,0:T(8,128)(2,1)S(1)} %get-tuple-element.81), channel_id=1, source_target_pairs={{0,2},{1,3},{2,4},{3,5},{4,6},{5,7},{6,0},{7,1},{8,10},{9,11},{10,... | collective-permute-start | bytes 638984 | tf_op jit(solution)/shard_map/ppermute | solution.py:35
  79.0 13.9 %collective-permute-start.12 = (bf16[64,1664]{1,0:T(8,128)(2,1)S(1)}, bf16[64,1664]{1,0:T(8,128)(2,1)S(1)}, u32[]{:S(2)}, u32[]{:S(2)}) collective-permute-start(bf16[64,1664]{1,0:T(8,128)(2,1)S(1)} %get-tuple-element.79), channel_id=1, source_target_pairs={{0,4},{1,5},{2,6},{3,7},{4,0},{5,1},{6,2},{7,3},{8,12},{9,13},{10,... | collective-permute-start | bytes 638984 | tf_op jit(solution)/shard_map/ppermute | solution.py:35
  93.1 100.2 %all-gather.14.cloned.1.call-start = ((), (), s32[]{:S(2)}) async-start(), calls=%async_computation.3 | async-start | bytes 3461120 | tf_op jit(solution)/shard_map/all_gather | solution.py:110
  93.2 7.8 %collective-permute-start.45 = (bf16[416,208]{1,0:T(8,128)(2,1)S(1)}, bf16[416,208]{1,0:T(8,128)(2,1)S(1)}, u32[]{:S(2)}, u32[]{:S(2)}) collective-permute-start(bf16[416,208]{1,0:T(8,128)(2,1)S(1)} %copy-done.5), channel_id=1, source_target_pairs={{0,8},{8,0},{16,24},{24,16},{1,9},{9,1},{17,25},{25,17},{2,10},{10... | collective-permute-start | bytes 519176 | tf_op jit(solution)/shard_map/ppermute | solution.py:102
  102.2 22.3 %collective-permute-start.17 = (bf16[64,1664]{1,0:T(8,128)(2,1)S(1)}, bf16[64,1664]{1,0:T(8,128)(2,1)S(1)}, u32[]{:S(2)}, u32[]{:S(2)}) collective-permute-start(bf16[64,1664]{1,0:T(8,128)(2,1)S(1)} %get-tuple-element.51), channel_id=1, source_target_pairs={{0,1},{1,0},{2,3},{3,2},{4,5},{5,4},{6,7},{7,6},{8,9},{9,8},{10,11... | collective-permute-start | bytes 638984 | tf_op jit(solution)/shard_map/ppermute | solution.py:35
  102.8 9.1 %collective-permute-start.18 = (bf16[64,1664]{1,0:T(8,128)(2,1)S(1)}, bf16[64,1664]{1,0:T(8,128)(2,1)S(1)}, u32[]{:S(2)}, u32[]{:S(2)}) collective-permute-start(bf16[64,1664]{1,0:T(8,128)(2,1)S(1)} %get-tuple-element.51), channel_id=1, source_target_pairs={{0,6},{1,7},{2,0},{3,1},{4,2},{5,3},{6,4},{7,5},{8,14},{9,15},{10,... | collective-permute-start | bytes 638984 | tf_op jit(solution)/shard_map/ppermute | solution.py:35
  104.8 17.7 %collective-permute-start.20 = (bf16[64,1664]{1,0:T(8,128)(2,1)S(1)}, bf16[64,1664]{1,0:T(8,128)(2,1)S(1)}, u32[]{:S(2)}, u32[]{:S(2)}) collective-permute-start(bf16[64,1664]{1,0:T(8,128)(2,1)S(1)} %get-tuple-element.51), channel_id=1, source_target_pairs={{0,4},{1,5},{2,6},{3,7},{4,0},{5,1},{6,2},{7,3},{8,12},{9,13},{10,... | collective-permute-start | bytes 638984 | tf_op jit(solution)/shard_map/ppermute | solution.py:35
  104.8 19.2 %collective-permute-start.22 = (bf16[64,1664]{1,0:T(8,128)(2,1)S(1)}, bf16[64,1664]{1,0:T(8,128)(2,1)S(1)}, u32[]{:S(2)}, u32[]{:S(2)}) collective-permute-start(bf16[64,1664]{1,0:T(8,128)(2,1)S(1)} %get-tuple-element.51), channel_id=1, source_target_pairs={{0,2},{1,3},{2,4},{3,5},{4,6},{5,7},{6,0},{7,1},{8,10},{9,11},{10,... | collective-permute-start | bytes 638984 | tf_op jit(solution)/shard_map/ppermute | solution.py:35
  111.9 14.1 %collective-permute-start.19 = (bf16[64,1664]{1,0:T(8,128)(2,1)S(1)}, bf16[64,1664]{1,0:T(8,128)(2,1)S(1)}, u32[]{:S(2)}, u32[]{:S(2)}) collective-permute-start(bf16[64,1664]{1,0:T(8,128)(2,1)S(1)} %collective-permute-done.18), channel_id=1, source_target_pairs={{0,1},{1,0},{2,3},{3,2},{4,5},{5,4},{6,7},{7,6},{8,9},{9,8},{10,11... | collective-permute-start | bytes 638984 | tf_op jit(solution)/shard_map/ppermute | solution.py:35
  122.5 8.2 %collective-permute-start.21 = (bf16[64,1664]{1,0:T(8,128)(2,1)S(1)}, bf16[64,1664]{1,0:T(8,128)(2,1)S(1)}, u32[]{:S(2)}, u32[]{:S(2)}) collective-permute-start(bf16[64,1664]{1,0:T(8,128)(2,1)S(1)} %collective-permute-done.20), channel_id=1, source_target_pairs={{0,1},{1,0},{2,3},{3,2},{4,5},{5,4},{6,7},{7,6},{8,9},{9,8},{10,11... | collective-permute-start | bytes 638984 | tf_op jit(solution)/shard_map/ppermute | solution.py:35
  124.0 9.9 %collective-permute-start.23 = (bf16[64,1664]{1,0:T(8,128)(2,1)S(1)}, bf16[64,1664]{1,0:T(8,128)(2,1)S(1)}, u32[]{:S(2)}, u32[]{:S(2)}) collective-permute-start(bf16[64,1664]{1,0:T(8,128)(2,1)S(1)} %collective-permute-done.22), channel_id=1, source_target_pairs={{0,1},{1,0},{2,3},{3,2},{4,5},{5,4},{6,7},{7,6},{8,9},{9,8},{10,11... | collective-permute-start | bytes 638984 | tf_op jit(solution)/shard_map/ppermute | solution.py:35
  134.6 29.1 %collective-permute-start.38 = (bf16[80,1664]{1,0:T(8,128)(2,1)}, bf16[80,1664]{1,0:T(8,128)(2,1)}, u32[]{:S(2)}, u32[]{:S(2)}) collective-permute-start(bf16[80,1664]{1,0:T(8,128)(2,1)} %param.15), channel_id=1, source_target_pairs={{0,1},{1,0},{2,3},{3,2},{4,5},{5,4},{6,7},{7,6},{8,9},{9,8},{10,11... | collective-permute-start | bytes 798728 | tf_op jit(solution)/shard_map/ppermute | solution.py:35
  136.0 34.6 %collective-permute-start.39 = (bf16[80,1664]{1,0:T(8,128)(2,1)}, bf16[80,1664]{1,0:T(8,128)(2,1)}, u32[]{:S(2)}, u32[]{:S(2)}) collective-permute-start(bf16[80,1664]{1,0:T(8,128)(2,1)} %param.15), channel_id=1, source_target_pairs={{0,6},{1,7},{2,0},{3,1},{4,2},{5,3},{6,4},{7,5},{8,14},{9,15},{10,... | collective-permute-start | bytes 798728 | tf_op jit(solution)/shard_map/ppermute | solution.py:35
  136.0 85.6 %all-gather.16.cloned.1.call-start = ((), (), s32[]{:S(2)}) async-start(), calls=%async_computation.4 | async-start | bytes 2662400 | tf_op jit(solution)/shard_map/all_gather | solution.py:110
  148.1 8.3 %collective-permute-start.25 = (bf16[64,1664]{1,0:T(8,128)(2,1)S(1)}, bf16[64,1664]{1,0:T(8,128)(2,1)S(1)}, u32[]{:S(2)}, u32[]{:S(2)}) collective-permute-start(bf16[64,1664]{1,0:T(8,128)(2,1)S(1)} %get-tuple-element.71), channel_id=1, source_target_pairs={{0,1},{1,0},{2,3},{3,2},{4,5},{5,4},{6,7},{7,6},{8,9},{9,8},{10,11... | collective-permute-start | bytes 638984 | tf_op jit(solution)/shard_map/ppermute | solution.py:35
  148.8 11.9 %collective-permute-start.29 = (bf16[64,1664]{1,0:T(8,128)(2,1)S(1)}, bf16[64,1664]{1,0:T(8,128)(2,1)S(1)}, u32[]{:S(2)}, u32[]{:S(2)}) collective-permute-start(bf16[64,1664]{1,0:T(8,128)(2,1)S(1)} %get-tuple-element.69), channel_id=1, source_target_pairs={{0,1},{1,0},{2,3},{3,2},{4,5},{5,4},{6,7},{7,6},{8,9},{9,8},{10,11... | collective-permute-start | bytes 638984 | tf_op jit(solution)/shard_map/ppermute | solution.py:35
  150.2 12.7 %collective-permute-start.27 = (bf16[64,1664]{1,0:T(8,128)(2,1)S(1)}, bf16[64,1664]{1,0:T(8,128)(2,1)S(1)}, u32[]{:S(2)}, u32[]{:S(2)}) collective-permute-start(bf16[64,1664]{1,0:T(8,128)(2,1)S(1)} %get-tuple-element.70), channel_id=1, source_target_pairs={{0,1},{1,0},{2,3},{3,2},{4,5},{5,4},{6,7},{7,6},{8,9},{9,8},{10,11... | collective-permute-start | bytes 638984 | tf_op jit(solution)/shard_map/ppermute | solution.py:35
  156.4 27.8 %collective-permute-start.41 = (bf16[80,1664]{1,0:T(8,128)(2,1)}, bf16[80,1664]{1,0:T(8,128)(2,1)}, u32[]{:S(2)}, u32[]{:S(2)}) collective-permute-start(bf16[80,1664]{1,0:T(8,128)(2,1)} %param.15), channel_id=1, source_target_pairs={{0,4},{1,5},{2,6},{3,7},{4,0},{5,1},{6,2},{7,3},{8,12},{9,13},{10,... | collective-permute-start | bytes 798728 | tf_op jit(solution)/shard_map/ppermute | solution.py:35
  160.6 24.2 %collective-permute-start.43 = (bf16[80,1664]{1,0:T(8,128)(2,1)}, bf16[80,1664]{1,0:T(8,128)(2,1)}, u32[]{:S(2)}, u32[]{:S(2)}) collective-permute-start(bf16[80,1664]{1,0:T(8,128)(2,1)} %param.15), channel_id=1, source_target_pairs={{0,2},{1,3},{2,4},{3,5},{4,6},{5,7},{6,0},{7,1},{8,10},{9,11},{10,... | collective-permute-start | bytes 798728 | tf_op jit(solution)/shard_map/ppermute | solution.py:35
  163.7 22.6 %collective-permute-start.30 = (bf16[64,1664]{1,0:T(8,128)(2,1)S(1)}, bf16[64,1664]{1,0:T(8,128)(2,1)S(1)}, u32[]{:S(2)}, u32[]{:S(2)}) collective-permute-start(bf16[64,1664]{1,0:T(8,128)(2,1)S(1)} %get-tuple-element.73), channel_id=1, source_target_pairs={{0,6},{1,7},{2,0},{3,1},{4,2},{5,3},{6,4},{7,5},{8,14},{9,15},{10,... | collective-permute-start | bytes 638984 | tf_op jit(solution)/shard_map/ppermute | solution.py:35
  168.8 18.1 %collective-permute-start.28 = (bf16[64,1664]{1,0:T(8,128)(2,1)S(1)}, bf16[64,1664]{1,0:T(8,128)(2,1)S(1)}, u32[]{:S(2)}, u32[]{:S(2)}) collective-permute-start(bf16[64,1664]{1,0:T(8,128)(2,1)S(1)} %get-tuple-element.74), channel_id=1, source_target_pairs={{0,2},{1,3},{2,4},{3,5},{4,6},{5,7},{6,0},{7,1},{8,10},{9,11},{10,... | collective-permute-start | bytes 638984 | tf_op jit(solution)/shard_map/ppermute | solution.py:35
  170.6 20.2 %collective-permute-start.26 = (bf16[64,1664]{1,0:T(8,128)(2,1)S(1)}, bf16[64,1664]{1,0:T(8,128)(2,1)S(1)}, u32[]{:S(2)}, u32[]{:S(2)}) collective-permute-start(bf16[64,1664]{1,0:T(8,128)(2,1)S(1)} %get-tuple-element.72), channel_id=1, source_target_pairs={{0,4},{1,5},{2,6},{3,7},{4,0},{5,1},{6,2},{7,3},{8,12},{9,13},{10,... | collective-permute-start | bytes 638984 | tf_op jit(solution)/shard_map/ppermute | solution.py:35
  184.8 36.9 %collective-permute-start.42 = (bf16[80,1664]{1,0:T(8,128)(2,1)}, bf16[80,1664]{1,0:T(8,128)(2,1)}, u32[]{:S(2)}, u32[]{:S(2)}) collective-permute-start(bf16[80,1664]{1,0:T(8,128)(2,1)} %collective-permute-done.41), channel_id=1, source_target_pairs={{0,1},{1,0},{2,3},{3,2},{4,5},{5,4},{6,7},{7,6},{8,9},{9,8},{10,11... | collective-permute-start | bytes 798728 | tf_op jit(solution)/shard_map/ppermute | solution.py:35
  186.2 38.9 %collective-permute-start.44 = (bf16[80,1664]{1,0:T(8,128)(2,1)}, bf16[80,1664]{1,0:T(8,128)(2,1)}, u32[]{:S(2)}, u32[]{:S(2)}) collective-permute-start(bf16[80,1664]{1,0:T(8,128)(2,1)} %collective-permute-done.43), channel_id=1, source_target_pairs={{0,1},{1,0},{2,3},{3,2},{4,5},{5,4},{6,7},{7,6},{8,9},{9,8},{10,11... | collective-permute-start | bytes 798728 | tf_op jit(solution)/shard_map/ppermute | solution.py:35
  196.0 16.1 %collective-permute-start.34 = (bf16[16,6656]{1,0:T(8,128)(2,1)S(1)}, bf16[16,6656]{1,0:T(8,128)(2,1)S(1)}, u32[]{:S(2)}, u32[]{:S(2)}) collective-permute-start(bf16[16,6656]{1,0:T(8,128)(2,1)S(1)} %reshape.368), channel_id=1, source_target_pairs={{0,4},{1,5},{2,6},{3,7},{4,0},{5,1},{6,2},{7,3},{8,12},{9,13},{10,... | collective-permute-start | bytes 638984 | tf_op jit(solution)/shard_map/ppermute | solution.py:35
  196.1 112.5 %all-gather.18.cloned.1.call-start = ((), (), s32[]{:S(2)}) async-start(), calls=%async_computation.5 | async-start | bytes 4259840 | tf_op jit(solution)/shard_map/all_gather | solution.py:110
  201.2 12.3 %collective-permute-start.36 = (bf16[16,6656]{1,0:T(8,128)(2,1)S(1)}, bf16[16,6656]{1,0:T(8,128)(2,1)S(1)}, u32[]{:S(2)}, u32[]{:S(2)}) collective-permute-start(bf16[16,6656]{1,0:T(8,128)(2,1)S(1)} %reshape.368), channel_id=1, source_target_pairs={{0,2},{1,3},{2,4},{3,5},{4,6},{5,7},{6,0},{7,1},{8,10},{9,11},{10,... | collective-permute-start | bytes 638984 | tf_op jit(solution)/shard_map/ppermute | solution.py:35
  201.8 12.3 %collective-permute-start.33 = (bf16[16,6656]{1,0:T(8,128)(2,1)}, bf16[16,6656]{1,0:T(8,128)(2,1)S(1)}, u32[]{:S(2)}, u32[]{:S(2)}) collective-permute-start(bf16[16,6656]{1,0:T(8,128)(2,1)} %collective-permute-done.32), channel_id=1, source_target_pairs={{0,1},{1,0},{2,3},{3,2},{4,5},{5,4},{6,7},{7,6},{8,9},{9,8},{10,11... | collective-permute-start | bytes 638984 | tf_op jit(solution)/shard_map/ppermute | solution.py:35
  221.7 116.6 %all-gather.20.cloned.1.call-start = ((), (), s32[]{:S(2)}) async-start(), calls=%async_computation.6 | async-start | bytes 4259840 | tf_op jit(solution)/shard_map/all_gather | solution.py:110
  270.1 8.3 %collective-permute-start.49 = (bf16[80,1664]{1,0:T(8,128)(2,1)S(1)}, bf16[80,1664]{1,0:T(8,128)(2,1)S(1)}, u32[]{:S(2)}, u32[]{:S(2)}) collective-permute-start(bf16[80,1664]{1,0:T(8,128)(2,1)S(1)} %get-tuple-element.64), channel_id=1, source_target_pairs={{0,1},{1,0},{2,3},{3,2},{4,5},{5,4},{6,7},{7,6},{8,9},{9,8},{10,11... | collective-permute-start | bytes 798728 | tf_op jit(solution)/shard_map/ppermute | solution.py:35
  270.1 11.0 %collective-permute-start.53 = (bf16[80,1664]{1,0:T(8,128)(2,1)S(1)}, bf16[80,1664]{1,0:T(8,128)(2,1)S(1)}, u32[]{:S(2)}, u32[]{:S(2)}) collective-permute-start(bf16[80,1664]{1,0:T(8,128)(2,1)S(1)} %get-tuple-element.62), channel_id=1, source_target_pairs={{0,1},{1,0},{2,3},{3,2},{4,5},{5,4},{6,7},{7,6},{8,9},{9,8},{10,11... | collective-permute-start | bytes 798728 | tf_op jit(solution)/shard_map/ppermute | solution.py:35
  272.1 11.9 %collective-permute-start.51 = (bf16[80,1664]{1,0:T(8,128)(2,1)S(1)}, bf16[80,1664]{1,0:T(8,128)(2,1)S(1)}, u32[]{:S(2)}, u32[]{:S(2)}) collective-permute-start(bf16[80,1664]{1,0:T(8,128)(2,1)S(1)} %get-tuple-element.63), channel_id=1, source_target_pairs={{0,1},{1,0},{2,3},{3,2},{4,5},{5,4},{6,7},{7,6},{8,9},{9,8},{10,11... | collective-permute-start | bytes 798728 | tf_op jit(solution)/shard_map/ppermute | solution.py:35
  272.2 15.2 %collective-permute-start.48 = (bf16[80,1664]{1,0:T(8,128)(2,1)S(1)}, bf16[80,1664]{1,0:T(8,128)(2,1)S(1)}, u32[]{:S(2)}, u32[]{:S(2)}) collective-permute-start(bf16[80,1664]{1,0:T(8,128)(2,1)S(1)} %get-tuple-element.61), channel_id=1, source_target_pairs={{0,1},{1,0},{2,3},{3,2},{4,5},{5,4},{6,7},{7,6},{8,9},{9,8},{10,11... | collective-permute-start | bytes 798728 | tf_op jit(solution)/shard_map/ppermute | solution.py:35
  284.2 11.0 %collective-permute-start.54 = (bf16[80,1664]{1,0:T(8,128)(2,1)S(1)}, bf16[80,1664]{1,0:T(8,128)(2,1)S(1)}, u32[]{:S(2)}, u32[]{:S(2)}) collective-permute-start(bf16[80,1664]{1,0:T(8,128)(2,1)S(1)} %get-tuple-element.66), channel_id=1, source_target_pairs={{0,6},{1,7},{2,0},{3,1},{4,2},{5,3},{6,4},{7,5},{8,14},{9,15},{10,... | collective-permute-start | bytes 798728 | tf_op jit(solution)/shard_map/ppermute | solution.py:35
  286.8 9.6 %collective-permute-start.52 = (bf16[80,1664]{1,0:T(8,128)(2,1)S(1)}, bf16[80,1664]{1,0:T(8,128)(2,1)S(1)}, u32[]{:S(2)}, u32[]{:S(2)}) collective-permute-start(bf16[80,1664]{1,0:T(8,128)(2,1)S(1)} %get-tuple-element.67), channel_id=1, source_target_pairs={{0,2},{1,3},{2,4},{3,5},{4,6},{5,7},{6,0},{7,1},{8,10},{9,11},{10,... | collective-permute-start | bytes 798728 | tf_op jit(solution)/shard_map/ppermute | solution.py:35
  286.8 20.6 %collective-permute-start.50 = (bf16[80,1664]{1,0:T(8,128)(2,1)S(1)}, bf16[80,1664]{1,0:T(8,128)(2,1)S(1)}, u32[]{:S(2)}, u32[]{:S(2)}) collective-permute-start(bf16[80,1664]{1,0:T(8,128)(2,1)S(1)} %get-tuple-element.65), channel_id=1, source_target_pairs={{0,4},{1,5},{2,6},{3,7},{4,0},{5,1},{6,2},{7,3},{8,12},{9,13},{10,... | collective-permute-start | bytes 798728 | tf_op jit(solution)/shard_map/ppermute | solution.py:35
  312.4 13.0 %collective-permute-start.58 = (bf16[80,1664]{1,0:T(8,128)(2,1)S(1)}, bf16[80,1664]{1,0:T(8,128)(2,1)S(1)}, u32[]{:S(2)}, u32[]{:S(2)}) collective-permute-start(bf16[80,1664]{1,0:T(8,128)(2,1)S(1)} %get-tuple-element.49), channel_id=1, source_target_pairs={{0,4},{1,5},{2,6},{3,7},{4,0},{5,1},{6,2},{7,3},{8,12},{9,13},{10,... | collective-permute-start | bytes 798728 | tf_op jit(solution)/shard_map/ppermute | solution.py:35
  312.4 14.5 %collective-permute-start.60 = (bf16[80,1664]{1,0:T(8,128)(2,1)S(1)}, bf16[80,1664]{1,0:T(8,128)(2,1)S(1)}, u32[]{:S(2)}, u32[]{:S(2)}) collective-permute-start(bf16[80,1664]{1,0:T(8,128)(2,1)S(1)} %get-tuple-element.49), channel_id=1, source_target_pairs={{0,2},{1,3},{2,4},{3,5},{4,6},{5,7},{6,0},{7,1},{8,10},{9,11},{10,... | collective-permute-start | bytes 798728 | tf_op jit(solution)/shard_map/ppermute | solution.py:35
  313.2 14.2 %collective-permute-start.55 = (bf16[80,1664]{1,0:T(8,128)(2,1)S(1)}, bf16[80,1664]{1,0:T(8,128)(2,1)S(1)}, u32[]{:S(2)}, u32[]{:S(2)}) collective-permute-start(bf16[80,1664]{1,0:T(8,128)(2,1)S(1)} %get-tuple-element.49), channel_id=1, source_target_pairs={{0,1},{1,0},{2,3},{3,2},{4,5},{5,4},{6,7},{7,6},{8,9},{9,8},{10,11... | collective-permute-start | bytes 798728 | tf_op jit(solution)/shard_map/ppermute | solution.py:35
  316.4 12.5 %collective-permute-start.57 = (bf16[80,1664]{1,0:T(8,128)(2,1)S(1)}, bf16[80,1664]{1,0:T(8,128)(2,1)S(1)}, u32[]{:S(2)}, u32[]{:S(2)}) collective-permute-start(bf16[80,1664]{1,0:T(8,128)(2,1)S(1)} %collective-permute-done.56), channel_id=1, source_target_pairs={{0,1},{1,0},{2,3},{3,2},{4,5},{5,4},{6,7},{7,6},{8,9},{9,8},{10,11... | collective-permute-start | bytes 798728 | tf_op jit(solution)/shard_map/ppermute | solution.py:35
  351.9 9.3 %collective-permute-start.63 = (bf16[80,1664]{1,0:T(8,128)(2,1)S(1)}, bf16[80,1664]{1,0:T(8,128)(2,1)S(1)}, u32[]{:S(2)}, u32[]{:S(2)}) collective-permute-start(bf16[80,1664]{1,0:T(8,128)(2,1)S(1)} %get-tuple-element.57), channel_id=1, source_target_pairs={{0,1},{1,0},{2,3},{3,2},{4,5},{5,4},{6,7},{7,6},{8,9},{9,8},{10,11... | collective-permute-start | bytes 798728 | tf_op jit(solution)/shard_map/ppermute | solution.py:35
  353.4 13.5 %collective-permute-start.67 = (bf16[80,1664]{1,0:T(8,128)(2,1)S(1)}, bf16[80,1664]{1,0:T(8,128)(2,1)S(1)}, u32[]{:S(2)}, u32[]{:S(2)}) collective-permute-start(bf16[80,1664]{1,0:T(8,128)(2,1)S(1)} %get-tuple-element.55), channel_id=1, source_target_pairs={{0,1},{1,0},{2,3},{3,2},{4,5},{5,4},{6,7},{7,6},{8,9},{9,8},{10,11... | collective-permute-start | bytes 798728 | tf_op jit(solution)/shard_map/ppermute | solution.py:35
  354.0 18.6 %collective-permute-start.65 = (bf16[80,1664]{1,0:T(8,128)(2,1)S(1)}, bf16[80,1664]{1,0:T(8,128)(2,1)S(1)}, u32[]{:S(2)}, u32[]{:S(2)}) collective-permute-start(bf16[80,1664]{1,0:T(8,128)(2,1)S(1)} %get-tuple-element.56), channel_id=1, source_target_pairs={{0,1},{1,0},{2,3},{3,2},{4,5},{5,4},{6,7},{7,6},{8,9},{9,8},{10,11... | collective-permute-start | bytes 798728 | tf_op jit(solution)/shard_map/ppermute | solution.py:35
  355.4 22.2 %collective-permute-start.62 = (bf16[80,1664]{1,0:T(8,128)(2,1)S(1)}, bf16[80,1664]{1,0:T(8,128)(2,1)S(1)}, u32[]{:S(2)}, u32[]{:S(2)}) collective-permute-start(bf16[80,1664]{1,0:T(8,128)(2,1)S(1)} %get-tuple-element.54), channel_id=1, source_target_pairs={{0,1},{1,0},{2,3},{3,2},{4,5},{5,4},{6,7},{7,6},{8,9},{9,8},{10,11... | collective-permute-start | bytes 798728 | tf_op jit(solution)/shard_map/ppermute | solution.py:35
  372.8 10.2 %collective-permute-start.68 = (bf16[80,1664]{1,0:T(8,128)(2,1)S(1)}, bf16[80,1664]{1,0:T(8,128)(2,1)S(1)}, u32[]{:S(2)}, u32[]{:S(2)}) collective-permute-start(bf16[80,1664]{1,0:T(8,128)(2,1)S(1)} %get-tuple-element.59), channel_id=1, source_target_pairs={{0,6},{1,7},{2,0},{3,1},{4,2},{5,3},{6,4},{7,5},{8,14},{9,15},{10,... | collective-permute-start | bytes 798728 | tf_op jit(solution)/shard_map/ppermute | solution.py:35
  376.2 13.6 %collective-permute-start.66 = (bf16[80,1664]{1,0:T(8,128)(2,1)S(1)}, bf16[80,1664]{1,0:T(8,128)(2,1)S(1)}, u32[]{:S(2)}, u32[]{:S(2)}) collective-permute-start(bf16[80,1664]{1,0:T(8,128)(2,1)S(1)} %get-tuple-element.60), channel_id=1, source_target_pairs={{0,2},{1,3},{2,4},{3,5},{4,6},{5,7},{6,0},{7,1},{8,10},{9,11},{10,... | collective-permute-start | bytes 798728 | tf_op jit(solution)/shard_map/ppermute | solution.py:35
  376.2 21.7 %collective-permute-start.64 = (bf16[80,1664]{1,0:T(8,128)(2,1)S(1)}, bf16[80,1664]{1,0:T(8,128)(2,1)S(1)}, u32[]{:S(2)}, u32[]{:S(2)}) collective-permute-start(bf16[80,1664]{1,0:T(8,128)(2,1)S(1)} %get-tuple-element.58), channel_id=1, source_target_pairs={{0,4},{1,5},{2,6},{3,7},{4,0},{5,1},{6,2},{7,3},{8,12},{9,13},{10,... | collective-permute-start | bytes 798728 | tf_op jit(solution)/shard_map/ppermute | solution.py:35
  (21 other events, 308.5 us)
Sparse Core Ops, SparseCore 0:
  9.7 24.6 all-gather.7
  53.1 26.3 all-gather.9
  93.3 27.8 all-gather.11
  136.2 24.1 all-gather.13
  196.2 22.5 all-gather.15
  221.8 29.2 all-gather.17
  308.8 29.4 all-gather.19
